TPU v7x, 32 devices: a whole 2x2x4 slice. The times are simulated.
32 devices in a mesh: dp: 8 (over z, y), expert: 4 (over x, core).
Axes of the slice: x: 2, y: 2, z: 4, core: 2. Of those that a mesh axis runs over, the one named last changes fastest.
Arguments:
- tokens: bfloat16 [4096, 3584], P(('dp', 'expert')), may hold values from -6 to 6
- routes: int32 [4096, 1], P(('dp', 'expert')), may hold values from 0 to 3; in each aligned block of 128 rows (0 to 127, 128 to 255, ...) at most 48 rows name the same one
- gates: float32 [4096, 1], P(('dp', 'expert')), may hold values from 0.1 to 1
- counts: int32 [32], P(('dp', 'expert')), may hold values from 16 to 128, as said below
- expert_weight: bfloat16 [4, 3584, 1024], P('expert'), may hold values from -0.09375 to 0.09375
- cotangent: bfloat16 [4096, 1024], P(('dp', 'expert')), may hold values from -6 to 6
Outputs:
- mixed: bfloat16 [4096, 1024], P(('dp', 'expert'))
- token_grad: bfloat16 [4096, 3584], P(('dp', 'expert'))
- gate_grad: float32 [4096, 1], P(('dp', 'expert'))
Inputs may be any that keep to these rules, and one draw needn't show every extreme that they name: `routes`: among the tokens of one device at most 48 name one expert; some device sends exactly 48 to some expert; every expert is named. The first counts[i] tokens of device i are valid; some device has all of its tokens valid.
All inputs are finite; a program needn't handle non-finite values.
Results may differ from a plain program's by a relative error of at most 0.0058.
Values may be sent and summed in bfloat16 or wider, within the bound.
A program may use at most 64 MiB of HBM per device.

v0:
```python
import jax
import jax.numpy as jnp
from jax import lax
from jax.sharding import PartitionSpec as P


def forward_rows(inputs, weight):
    pre = jnp.einsum("skd,dh->skh", inputs, weight, preferred_element_type=jnp.float32)
    sig = jax.nn.sigmoid(pre)
    act = (pre * sig).astype(jnp.bfloat16)
    slope = sig * (1.0 + pre * (1.0 - sig))
    return (act, slope)


def backward_rows(upstream, slope, weight):
    delta = (upstream.astype(jnp.float32) * slope).astype(jnp.bfloat16)
    return jnp.einsum("skh,dh->skd", delta, weight, preferred_element_type=jnp.float32).astype(
        jnp.bfloat16
    )


def shards(tokens, routes, gates, counts, expert_weight, cotangent):
    local_rows = tokens.shape[0]
    experts_here = lax.axis_size("expert")
    capacity = 3 * local_rows // (2 * experts_here)
    slots_all = experts_here * capacity
    route = routes[:, 0]
    gate = gates[:, 0]
    weight = expert_weight[0]
    choose = (route[:, None] == jnp.arange(experts_here, dtype=jnp.int32)[None, :]).astype(
        jnp.int32
    )
    running = jnp.cumsum(choose, axis=0)
    rank = jnp.sum(running * choose, axis=1) - 1
    target = route * capacity + rank
    placing = (jnp.arange(slots_all, dtype=jnp.int32)[:, None] == target[None, :]).astype(
        jnp.bfloat16
    )
    position = jnp.arange(local_rows, dtype=jnp.int32)
    valid = (position < counts[0]).astype(jnp.float32)
    total = lax.psum(counts.astype(jnp.float32), ("dp", "expert"))[0]
    scale = jnp.float32(local_rows * lax.axis_size("dp") * experts_here) / total
    factor = valid * scale
    upstream = ((gate * factor)[:, None] * cotangent.astype(jnp.float32)).astype(jnp.bfloat16)
    outgoing = jnp.dot(placing, tokens, preferred_element_type=jnp.float32).astype(jnp.bfloat16)
    outgoing = outgoing.reshape(experts_here, capacity, tokens.shape[1])
    sending = jnp.dot(placing, upstream, preferred_element_type=jnp.float32).astype(jnp.bfloat16)
    sending = sending.reshape(experts_here, capacity, upstream.shape[1])
    act_slots, slope_slots = forward_rows(
        lax.all_to_all(outgoing, "expert", split_axis=0, concat_axis=0, tiled=True), weight
    )
    act_home = lax.all_to_all(act_slots, "expert", split_axis=0, concat_axis=0, tiled=True)
    arrived = lax.all_to_all(sending, "expert", split_axis=0, concat_axis=0, tiled=True)
    grad_slots = backward_rows(arrived, slope_slots, weight)
    grad_home = lax.all_to_all(grad_slots, "expert", split_axis=0, concat_axis=0, tiled=True)
    unplace = (((0,), (0,)), ((), ()))
    act_flat = act_home.reshape(slots_all, act_home.shape[2])
    grad_flat = grad_home.reshape(slots_all, grad_home.shape[2])
    act_float = lax.dot_general(placing, act_flat, unplace, preferred_element_type=jnp.float32)
    token_grad = lax.dot_general(
        placing, grad_flat, unplace, preferred_element_type=jnp.float32
    ).astype(jnp.bfloat16)
    mixed = (gate[:, None] * act_float).astype(jnp.bfloat16)
    gate_grad = (jnp.sum(act_float * cotangent.astype(jnp.float32), axis=1) * factor)[:, None]
    return (mixed, token_grad, gate_grad)


def solution(mesh):
    placed = (
        P(("dp", "expert"), None),
        P(("dp", "expert"), None),
        P(("dp", "expert"), None),
        P(("dp", "expert")),
        P("expert", None, None),
        P(("dp", "expert"), None),
    )
    return jax.shard_map(
        shards,
        mesh=mesh,
        in_specs=placed,
        out_specs=(P(("dp", "expert"), None), P(("dp", "expert"), None), P(("dp", "expert"), None)),
        check_vma=False,
    )
```

profile of v0, /device:TPU:1, one launch (start us, length us, event | category | flops | bytes accessed | tf_op | source)
XLA Modules:
  0.0 107.9 jit_solution(14876809217694720387)
XLA Ops:
  0.6 0.0 copy-start
  0.6 0.8 fusion.13
  1.5 0.2 reduce_window_sum.11
  1.6 0.8 select_reduce_fusion
  2.5 0.7 add_add_fusion
  3.1 0.0 copy-done
  3.1 1.6 %convolution_convert_fusion = bf16[192,3584]{1,0:T(8,128)(2,1)} fusion(bf16[128,3584]{1,0:T(8,128)(2,1)S(1)} %copy-done, s32[128]{0:T(128)S(1)} %add_add_fusion), kind=kOutput, calls=%fused_computation.5 | convolution fusion | flops 176873472 | bytes 2294272 | tf_op jit(solution)/shard_map/dot_general | solution.py:45
  4.7 0.0 copy-start.2
  4.7 0.0 copy-start.1
  4.7 4.4 %all-to-all-start = ((bf16[4,48,3584]{2,1,0:T(8,128)(2,1)}), bf16[4,48,3584]{2,1,0:T(8,128)(2,1)S(1)}, u32[]{:S(2)}, u32[]{:S(2)}) async-start(bf16[4,48,3584]{2,1,0:T(8,128)(2,1)} %bitcast.2), calls=%async_computation | async-start | bytes 2752512 | tf_op jit(solution)/shard_map/all_to_all | solution.py:50
  9.8 51.2 %psum.7 = f32[1]{0:T(128)} all-reduce(f32[1]{0:T(128)S(6)} %convert_element_type.43), channel_id=1, replica_groups=mesh['dp'=8,'expert'=4] {'dp','expert'}, use_global_device_ids=true, to_apply=%region_2.3 | all-reduce | flops 1 | bytes 8 | tf_op jit(solution)/shard_map/psum | solution.py:41
  61.6 0.0 copy-done.2
  61.7 0.0 copy-done.1
  61.7 1.1 %convolution_convert_fusion.2 = bf16[192,1024]{1,0:T(8,128)(2,1)} fusion(bf16[128,1024]{1,0:T(8,128)(2,1)S(1)} %copy-done.1, f32[128]{0:T(128)S(1)} %multiply_bitcast_fusion, s32[128]{0:T(128)S(1)} %add_add_fusion), kind=kOutput, calls=%fused_computation.7 | convolution fusion | flops 50946048 | bytes 656384 | tf_op jit(solution)/shard_map/dot_general | solution.py:47
  62.8 0.0 all-to-all-done
  62.8 4.8 %all-to-all-start.2 = ((bf16[4,48,1024]{2,1,0:T(8,128)(2,1)}), bf16[4,48,1024]{2,1,0:T(8,128)(2,1)S(1)}, u32[]{:S(2)}, u32[]{:S(2)}) async-start(bf16[4,48,1024]{2,1,0:T(8,128)(2,1)} %bitcast.9), calls=%async_computation.2 | async-start | bytes 786432 | tf_op jit(solution)/shard_map/all_to_all | solution.py:53
  67.6 5.7 %multiply_convert_fusion.1 = (bf16[4,48,1024]{2,1,0:T(8,128)(2,1)}, f32[4,48,1024]{2,1,0:T(8,128)}) fusion(bf16[4,48,3584]{2,1,0:T(8,128)(2,1)S(1)} %all-to-all-done, bf16[1,3584,1024]{2,1,0:T(8,128)(2,1)} %param.10), kind=kOutput, calls=%fused_computation.9 | convolution fusion | flops 1410269184 | bytes 9895936 | tf_op jit(solution)/shard_map/skd,dh->skh/dot_general | solution.py:8
  73.3 0.7 all-to-all-done.2
  74.0 4.5 %all-to-all-start.1 = ((bf16[4,48,1024]{2,1,0:T(8,128)(2,1)}), bf16[4,48,1024]{2,1,0:T(8,128)(2,1)S(1)}, u32[]{:S(2)}, u32[]{:S(2)}) async-start(bf16[4,48,1024]{2,1,0:T(8,128)(2,1)} %get-tuple-element.5), calls=%async_computation.1 | async-start | bytes 786432 | tf_op jit(solution)/shard_map/all_to_all | solution.py:52
  78.5 7.0 %fusion.4 = bf16[4,48,3584]{2,1,0:T(8,128)(2,1)} fusion(bf16[1,3584,1024]{2,1,0:T(8,128)(2,1)} %param.10, f32[4,48,1024]{2,1,0:T(8,128)} %get-tuple-element.6, bf16[4,48,1024]{2,1,0:T(8,128)(2,1)S(1)} %all-to-all-done.2), kind=kOutput, calls=%fused_computation.4 | convolution fusion | flops 1411940352 | bytes 9895936 | tf_op jit(solution)/shard_map/skh,dh->skd/dot_general | solution.py:17
  85.5 0.0 all-to-all-done.1
  85.5 3.9 %all-to-all-start.3 = ((bf16[4,48,3584]{2,1,0:T(8,128)(2,1)}), bf16[4,48,3584]{2,1,0:T(8,128)(2,1)S(1)}, u32[]{:S(2)}, u32[]{:S(2)}) async-start(bf16[4,48,3584]{2,1,0:T(8,128)(2,1)} %fusion.4), calls=%async_computation.3 | async-start | bytes 2752512 | tf_op jit(solution)/shard_map/all_to_all | solution.py:55
  89.4 1.1 fusion.8
  90.5 0.5 bitcast_multiply_fusion
  91.0 15.5 %all-to-all-done.3 = bf16[4,48,3584]{2,1,0:T(8,128)(2,1)S(1)} async-done(((bf16[4,48,3584]{2,1,0:T(8,128)(2,1)}), bf16[4,48,3584]{2,1,0:T(8,128)(2,1)S(1)}, u32[]{:S(2)}, u32[]{:S(2)}) %all-to-all-start.3) | async-done | bytes 1376288 | tf_op jit(solution)/shard_map/all_to_all | solution.py:55
  106.5 1.4 %convolution_convert_fusion.1 = bf16[128,3584]{1,0:T(8,128)(2,1)} fusion(bf16[192,3584]{1,0:T(8,128)(2,1)S(1)} %bitcast.29, s32[128]{0:T(128)S(1)} %add_add_fusion), kind=kOutput, calls=%fused_computation.6 | convolution fusion | flops 176644096 | bytes 2294272 | tf_op jit(solution)/shard_map/dot_general | solution.py:60
  (1 shorter events, 0.0 us)
Async XLA Ops:
  0.6 2.5 %copy-start = (bf16[128,3584]{1,0:T(8,128)(2,1)S(1)}, bf16[128,3584]{1,0:T(8,128)(2,1)}, u32[]{:S(2)}) copy-start(bf16[128,3584]{1,0:T(8,128)(2,1)} %param.6) | copy-start | bytes 2752516
  4.7 56.9 %copy-start.2 = (f32[128,1]{0,1:T(1,128)S(1)}, f32[128,1]{0,1:T(1,128)}, u32[]{:S(2)}) copy-start(f32[128,1]{0,1:T(1,128)} %param.8) | copy-start | bytes 1540
  4.7 56.9 %copy-start.1 = (bf16[128,1024]{1,0:T(8,128)(2,1)S(1)}, bf16[128,1024]{1,0:T(8,128)(2,1)}, u32[]{:S(2)}) copy-start(bf16[128,1024]{1,0:T(8,128)(2,1)} %param.11) | copy-start | bytes 786436
  4.7 58.0 %all-to-all-start = ((bf16[4,48,3584]{2,1,0:T(8,128)(2,1)}), bf16[4,48,3584]{2,1,0:T(8,128)(2,1)S(1)}, u32[]{:S(2)}, u32[]{:S(2)}) async-start(bf16[4,48,3584]{2,1,0:T(8,128)(2,1)} %bitcast.2), calls=%async_computation | async-start | bytes 2752512 | tf_op jit(solution)/shard_map/all_to_all | solution.py:50
  62.8 11.2 %all-to-all-start.2 = ((bf16[4,48,1024]{2,1,0:T(8,128)(2,1)}), bf16[4,48,1024]{2,1,0:T(8,128)(2,1)S(1)}, u32[]{:S(2)}, u32[]{:S(2)}) async-start(bf16[4,48,1024]{2,1,0:T(8,128)(2,1)} %bitcast.9), calls=%async_computation.2 | async-start | bytes 786432 | tf_op jit(solution)/shard_map/all_to_all | solution.py:53
  74.0 11.5 %all-to-all-start.1 = ((bf16[4,48,1024]{2,1,0:T(8,128)(2,1)}), bf16[4,48,1024]{2,1,0:T(8,128)(2,1)S(1)}, u32[]{:S(2)}, u32[]{:S(2)}) async-start(bf16[4,48,1024]{2,1,0:T(8,128)(2,1)} %get-tuple-element.5), calls=%async_computation.1 | async-start | bytes 786432 | tf_op jit(solution)/shard_map/all_to_all | solution.py:52
  85.5 21.0 %all-to-all-start.3 = ((bf16[4,48,3584]{2,1,0:T(8,128)(2,1)}), bf16[4,48,3584]{2,1,0:T(8,128)(2,1)S(1)}, u32[]{:S(2)}, u32[]{:S(2)}) async-start(bf16[4,48,3584]{2,1,0:T(8,128)(2,1)} %fusion.4), calls=%async_computation.3 | async-start | bytes 2752512 | tf_op jit(solution)/shard_map/all_to_all | solution.py:55
where the time goes:
time: 109 us; the launch traced here: 108 us
  blocking collectives  51.2 us (47%)
  matrix products  17.9 us (16%)
  starting transfers between devices  17.6 us (16%)
  waiting for transfers between devices  16.2 us (15%)
  other arithmetic  3 us (3%)
  between operations  2.03 us (2%)
    psum x1, blocking collectives, shards(): total = lax.psum(counts.astype(jnp.float32), ('dp', 'expert'))[0]  51.2 us
    all_to_all x1, waiting for transfers between devices, shards(): lax.all_to_all(grad_slots, 'expert', split_axis=0, concat_axis=0, tiled=T...  15.5 us
    dot_general x1, matrix products, backward_rows(): jnp.einsum('skh,dh->skd', delta, weight, preferred_element_type=jnp.float32)  7.03 us
    dot_general x1, matrix products, forward_rows(): jnp.einsum('skd,dh->skh', inputs, weight, preferred_element_type=jnp.floa...  5.71 us
    all_to_all x1, starting transfers between devices, shards(): lax.all_to_all(sending, 'expert', split_axis=0, concat_axis=0, tiled=True)  4.84 us
    all_to_all x1, starting transfers between devices, shards(): lax.all_to_all(act_slots, 'expert', split_axis=0, concat_axis=0, tiled=True)  4.47 us
    all_to_all x1, starting transfers between devices, shards(): lax.all_to_all(outgoing, 'expert', split_axis=0, concat_axis=0, tiled=True)  4.39 us
    all_to_all x1, starting transfers between devices, shards(): lax.all_to_all(grad_slots, 'expert', split_axis=0, concat_axis=0, tiled=T...  3.93 us
  transfers between devices with their start and end apart: 4, of which 2 were waited for; matrix products, arithmetic and copies ran while one was open for 14% of the time, Pallas kernels for 0%

commit v1 on v0

v1 whole, which is shorter than its diff:
```python
import functools

import jax
import jax.numpy as jnp
from jax import lax
from jax.experimental import pallas as pl
from jax.experimental.pallas import tpu as pltpu
from jax.sharding import PartitionSpec as P

MESH = pl.DeviceIdType.MESH
ROWS = 16
TOK, COT, ACT, GRAD = 0, 1, 2, 3


def tile_of(size, most):
    tile = most
    while size % tile:
        tile //= 2
    return tile


def kernel(
    n, groups, cap, routes_ref, gates_ref, counts_ref, tokens_hbm, weight_hbm, cotangent_hbm,
    mixed_hbm, grad_hbm, gate_grad_ref,
    tok, cot, w, place, unplace, tok_out, cot_out, tok_in, cot_in, delta,
    act_out, grad_out, act_home, grad_home, mixed_v, grad_v, cnt_mine, cnt_dp, cnt_sum, cnt_ex,
    load_sem, store_sem, send_sem, recv_sem, cnt_send, cnt_recv,
):
    rows, depth = tok.shape
    units = cot.shape[1]
    slots = n * cap
    pieces = cap // ROWS
    far = n - 2
    step = far * ROWS
    me = lax.axis_index("expert")
    group = lax.axis_index("dp")

    load_tok = pltpu.make_async_copy(tokens_hbm, tok, load_sem.at[0])
    load_cot = pltpu.make_async_copy(cotangent_hbm, cot, load_sem.at[1])
    load_w = pltpu.make_async_copy(weight_hbm.at[0], w, load_sem.at[2])
    load_tok.start()
    load_cot.start()
    load_w.start()

    barrier = pltpu.get_barrier_semaphore()
    for j in range(1, n):
        pl.semaphore_signal(
            barrier, inc=1, device_id=(group, lax.bitwise_xor(me, j)), device_id_type=MESH
        )
    for k in range(1, groups):
        pl.semaphore_signal(
            barrier, inc=1, device_id=(lax.rem(group + k, groups), me), device_id_type=MESH
        )

    route = routes_ref[...]
    high = -(-n // ROWS) * ROWS
    choose = lax.broadcasted_iota(jnp.int32, (high, rows), 0) == route
    choose_f = jnp.where(choose, 1.0, 0.0)
    upper = jnp.where(
        lax.broadcasted_iota(jnp.int32, (rows, rows), 0)
        <= lax.broadcasted_iota(jnp.int32, (rows, rows), 1),
        1.0,
        0.0,
    ).astype(jnp.bfloat16)
    running = jnp.dot(choose_f.astype(jnp.bfloat16), upper, preferred_element_type=jnp.float32)
    rank = (jnp.sum(running * choose_f, axis=0, keepdims=True) - 1.0).astype(jnp.int32)
    rel = lax.bitwise_xor(route, jnp.full(route.shape, me, jnp.int32))
    piece = lax.div(rank, jnp.int32(ROWS))
    slot = jnp.where(
        rel < 2,
        rel * cap + rank,
        2 * cap + piece * step + (rel - 2) * ROWS + (rank - piece * ROWS),
    )
    place[...] = jnp.where(
        lax.broadcasted_iota(jnp.int32, (slots, rows), 0) == slot, 1.0, 0.0
    ).astype(jnp.bfloat16)
    line = lax.broadcasted_iota(jnp.int32, (128, rows), 0)
    columns = jnp.transpose(
        jnp.where(line == 0, gates_ref[...], jnp.where(line == 1, slot.astype(jnp.float32), 0.0))
    )
    gate = columns[:, 0:1]
    unplace[...] = jnp.where(
        lax.broadcasted_iota(jnp.int32, (rows, slots), 1) == columns[:, 1:2].astype(jnp.int32),
        1.0,
        0.0,
    ).astype(jnp.bfloat16)
    count = counts_ref[0]
    cnt_mine[...] = jnp.full(cnt_mine.shape, count.astype(jnp.float32), jnp.float32)

    def remote(kind, source, target, j, part, at, size):
        return pltpu.make_async_remote_copy(
            src_ref=source.at[pl.ds(at, size)],
            dst_ref=target.at[pl.ds(at, size)],
            send_sem=send_sem.at[kind, j, part],
            recv_sem=recv_sem.at[kind, j, part],
            device_id=(group, lax.bitwise_xor(me, j)),
            device_id_type=MESH,
        )

    def gather(source, target, at, size):
        width = tile_of(source.shape[1], 512)

        def body(i, carry):
            cut = pl.ds(pl.multiple_of(i * width, width), width)
            target[at : at + size, cut] = jnp.dot(
                place[at : at + size, :], source[:, cut], preferred_element_type=jnp.float32
            ).astype(jnp.bfloat16)
            return carry

        lax.fori_loop(0, source.shape[1] // width, body, 0)

    def far_at(part, j):
        return 2 * cap + part * step + (j - 2) * ROWS

    out = []

    load_tok.wait()
    for part in range(pieces):
        gather(tok, tok_out, 2 * cap + part * step, step)
        if part == 0:
            load_cot.wait()
            pl.semaphore_wait(barrier, n - 1 + groups - 1)
        for j in range(2, n):
            copy = remote(TOK, tok_out, tok_in, j, part, far_at(part, j), ROWS)
            copy.start()
            out.append(copy)
        gather(cot, cot_out, 2 * cap + part * step, step)
        for j in range(2, n):
            copy = remote(COT, cot_out, cot_in, j, part, far_at(part, j), ROWS)
            copy.start()
            out.append(copy)
        if part == 0:
            gather(tok, tok_out, cap, cap)
            near_tok = remote(TOK, tok_out, tok_in, 1, 0, cap, cap)
            near_tok.start()
            gather(cot, cot_out, cap, cap)
            near_cot = remote(COT, cot_out, cot_in, 1, 0, cap, cap)
            near_cot.start()

    counts = []
    for k in range(1, groups):
        copy = pltpu.make_async_remote_copy(
            src_ref=cnt_mine,
            dst_ref=cnt_dp.at[k - 1],
            send_sem=cnt_send.at[k - 1],
            recv_sem=cnt_recv.at[k - 1],
            device_id=(lax.rem(group + k, groups), me),
            device_id_type=MESH,
        )
        copy.start()
        counts.append(copy)

    gather(tok, tok_in, 0, cap)
    gather(cot, cot_in, 0, cap)

    def forward(at, size, kept):
        width = tile_of(units, 256)

        def body(i, carry):
            cut = pl.ds(pl.multiple_of(i * width, width), width)
            pre = jnp.dot(
                tok_in[at : at + size, :], w[:, cut], preferred_element_type=jnp.float32
            )
            sig = jax.nn.sigmoid(pre)
            act = (pre * sig).astype(jnp.bfloat16)
            if kept:
                act_home[at : at + kept, cut] = act[:kept]
            act_out[at + kept : at + size, cut] = act[kept:]
            slope = sig * (1.0 + pre * (1.0 - sig))
            delta[0:size, cut] = (
                cot_in[at : at + size, cut].astype(jnp.float32) * slope
            ).astype(jnp.bfloat16)
            return carry

        lax.fori_loop(0, units // width, body, 0)

    def backward(at, size, kept):
        width = tile_of(depth, 512)

        def body(i, carry):
            cut = pl.ds(pl.multiple_of(i * width, width), width)
            grad = lax.dot_general(
                delta[0:size, :], w[cut, :], (((1,), (1,)), ((), ())),
                preferred_element_type=jnp.float32,
            ).astype(jnp.bfloat16)
            if kept:
                grad_home[at : at + kept, cut] = grad[:kept]
            grad_out[at + kept : at + size, cut] = grad[kept:]
            return carry

        lax.fori_loop(0, depth // width, body, 0)

    load_w.wait()
    near_tok.wait_recv()
    near_cot.wait_recv()
    forward(0, 2 * cap, cap)
    near_act = remote(ACT, act_out, act_home, 1, 0, cap, cap)
    near_act.start()
    backward(0, 2 * cap, cap)
    near_grad = remote(GRAD, grad_out, grad_home, 1, 0, cap, cap)
    near_grad.start()

    for copy in counts:
        copy.wait_recv()
    partial = cnt_mine[...]
    for k in range(1, groups):
        partial = partial + cnt_dp[k - 1]
    cnt_sum[...] = partial
    sums = []
    for j in range(1, n):
        copy = pltpu.make_async_remote_copy(
            src_ref=cnt_sum,
            dst_ref=cnt_ex.at[j - 1],
            send_sem=cnt_send.at[groups - 1 + j - 1],
            recv_sem=cnt_recv.at[groups - 1 + j - 1],
            device_id=(group, lax.bitwise_xor(me, j)),
            device_id_type=MESH,
        )
        copy.start()
        sums.append(copy)

    for part in range(pieces):
        at = 2 * cap + part * step
        for kind in (TOK, COT):
            for j in range(2, n):
                if kind == TOK:
                    remote(TOK, tok_out, tok_in, j, part, far_at(part, j), ROWS).wait_recv()
                else:
                    remote(COT, cot_out, cot_in, j, part, far_at(part, j), ROWS).wait_recv()
        forward(at, step, 0)
        for j in range(2, n):
            copy = remote(ACT, act_out, act_home, j, part, far_at(part, j), ROWS)
            copy.start()
        backward(at, step, 0)
        for j in range(2, n):
            copy = remote(GRAD, grad_out, grad_home, j, part, far_at(part, j), ROWS)
            copy.start()

    for copy in out:
        copy.wait_send()
    near_tok.wait_send()
    near_cot.wait_send()
    for copy in counts:
        copy.wait_send()
    for copy in sums:
        copy.wait()
    total = partial
    for j in range(1, n):
        total = total + cnt_ex[j - 1]
    scale = jnp.float32(rows * groups * n) / total[0:1, 0:1]
    position = lax.broadcasted_iota(jnp.int32, (rows, 1), 0)
    factor = jnp.where(position < count, 1.0, 0.0) * scale

    near_act.wait()
    for part in range(pieces):
        for j in range(2, n):
            remote(ACT, act_out, act_home, j, part, far_at(part, j), ROWS).wait()
    act = jnp.dot(unplace[...], act_home[...], preferred_element_type=jnp.float32)
    mixed_v[...] = (gate * act).astype(jnp.bfloat16)
    store_mixed = pltpu.make_async_copy(mixed_v, mixed_hbm, store_sem.at[0])
    store_mixed.start()
    dots = jnp.sum(act * cot[...].astype(jnp.float32), axis=1, keepdims=True) * factor
    gate_grad_ref[...] = jnp.transpose(jnp.broadcast_to(dots, (rows, 128)))[0:1, :]

    near_grad.wait()
    for part in range(pieces):
        for j in range(2, n):
            remote(GRAD, grad_out, grad_home, j, part, far_at(part, j), ROWS).wait()
    both = gate * factor
    width = tile_of(depth, 512)
    stores = []
    for i in range(depth // width):
        cut = pl.ds(i * width, width)
        grad_v[:, cut] = (
            jnp.dot(unplace[...], grad_home[:, cut], preferred_element_type=jnp.float32) * both
        ).astype(jnp.bfloat16)
        store = pltpu.make_async_copy(grad_v.at[:, cut], grad_hbm.at[:, cut], store_sem.at[1 + i])
        store.start()
        stores.append(store)
    store_mixed.wait()
    for store in stores:
        store.wait()


def solution(mesh):
    n = mesh.shape["expert"]
    groups = mesh.shape["dp"]

    def shards(tokens, routes, gates, counts, expert_weight, cotangent):
        rows, depth = tokens.shape
        units = cotangent.shape[1]
        cap = -(-(3 * rows // (2 * n)) // ROWS) * ROWS
        slots = n * cap
        pieces = cap // ROWS
        small = max(2 * cap, (n - 2) * ROWS)
        bf16 = jnp.bfloat16
        hbm = pl.BlockSpec(memory_space=pl.ANY)
        vmem = pl.BlockSpec(memory_space=pltpu.VMEM)
        mixed, token_grad, gate_grad = pl.pallas_call(
            functools.partial(kernel, n, groups, cap),
            out_shape=(
                jax.ShapeDtypeStruct((rows, units), bf16),
                jax.ShapeDtypeStruct((rows, depth), bf16),
                jax.ShapeDtypeStruct((1, rows), jnp.float32),
            ),
            in_specs=[vmem, vmem, pl.BlockSpec(memory_space=pltpu.SMEM), hbm, hbm, hbm],
            out_specs=(hbm, hbm, vmem),
            scratch_shapes=[
                pltpu.VMEM((rows, depth), bf16),
                pltpu.VMEM((rows, units), bf16),
                pltpu.VMEM((depth, units), bf16),
                pltpu.VMEM((slots, rows), bf16),
                pltpu.VMEM((rows, slots), bf16),
                pltpu.VMEM((slots, depth), bf16),
                pltpu.VMEM((slots, units), bf16),
                pltpu.VMEM((slots, depth), bf16),
                pltpu.VMEM((slots, units), bf16),
                pltpu.VMEM((small, units), bf16),
                pltpu.VMEM((slots, units), bf16),
                pltpu.VMEM((slots, depth), bf16),
                pltpu.VMEM((slots, units), bf16),
                pltpu.VMEM((slots, depth), bf16),
                pltpu.VMEM((rows, units), bf16),
                pltpu.VMEM((rows, depth), bf16),
                pltpu.VMEM((8, 128), jnp.float32),
                pltpu.VMEM((groups - 1, 8, 128), jnp.float32),
                pltpu.VMEM((8, 128), jnp.float32),
                pltpu.VMEM((n - 1, 8, 128), jnp.float32),
                pltpu.SemaphoreType.DMA((3,)),
                pltpu.SemaphoreType.DMA((1 + depth // tile_of(depth, 512),)),
                pltpu.SemaphoreType.DMA((4, n, pieces)),
                pltpu.SemaphoreType.DMA((4, n, pieces)),
                pltpu.SemaphoreType.DMA((groups - 1 + n - 1,)),
                pltpu.SemaphoreType.DMA((groups - 1 + n - 1,)),
            ],
            compiler_params=pltpu.CompilerParams(
                collective_id=0, has_side_effects=True, vmem_limit_bytes=48 * 1024 * 1024
            ),
        )(routes.reshape(1, rows), gates.reshape(1, rows), counts, tokens, expert_weight, cotangent)
        return (mixed, token_grad, gate_grad.reshape(rows, 1))

    spread = P(("dp", "expert"), None)
    return jax.shard_map(
        shards,
        mesh=mesh,
        in_specs=(spread, spread, spread, P(("dp", "expert")), P("expert", None, None), spread),
        out_specs=(spread, spread, spread),
        check_vma=False,
    )
```

time: 109 us -> 55.2 us (0.51)
  blocking collectives: 51.2 us -> 0 us
  Pallas kernels: 0 us -> 48.1 us
  matrix products: 17.9 us -> 0 us
  starting transfers between devices: 17.6 us -> 0 us
  waiting for transfers between devices: 16.2 us -> 0 us
  local copies, waits for them, and re-layouts: 0.02 us -> 5.57 us
  other arithmetic: 3 us -> 0 us
    psum x1 -> x0, blocking collectives: 51.2 us -> none  [shards(): total = lax.psum(counts.astype(jnp.float32), ('dp', 'expert'))[0]]
    pallas_call x0 -> x1, Pallas kernels: none -> 48.1 us  [shards(): pl.pallas_call(functools.partial(kernel, n, groups, cap), out_shape=(jax....]
    dot_general x6 -> x0, matrix products: 17.9 us -> none  [the longest x1 7.03 us: backward_rows(): jnp.einsum('skh,dh->skd', delta, weight, preferred_element_type=jnp.float32)]
    all_to_all x4 -> x0, starting transfers between devices: 17.6 us -> none  [the longest x1 4.84 us: shards(): lax.all_to_all(sending, 'expert', split_axis=0, concat_axis=0, tiled=True)]
    all_to_all x4 -> x0, waiting for transfers between devices: 16.2 us -> none  [the longest x1 15.5 us: shards(): lax.all_to_all(grad_slots, 'expert', split_axis=0, concat_axis=0, tiled=T...]
    unnamed x6 -> x11, local copies, waits for them, and re-layouts: 0.02 us -> 5.57 us
  transfers between devices with their start and end apart: 4 -> 0, of which waited for: 2 -> 0; matrix products, arithmetic and copies ran while one was open for 14% -> 0% of each run, Pallas kernels for 0% -> 0%
where the time goes in v1:
time: 55.2 us; the launch traced here: 55 us
  Pallas kernels  48.1 us (87%)
  local copies, waits for them, and re-layouts  5.57 us (10%)
  between operations  1.3 us (2%)
    pallas_call x1, Pallas kernels, shards(): pl.pallas_call(functools.partial(kernel, n, groups, cap), out_shape=(jax....  48.1 us
    unnamed x11, local copies, waits for them, and re-layouts  5.57 us

profile of v1, /device:TPU:1, one launch (start us, length us, event | category | flops | bytes accessed | tf_op | source)
XLA Modules:
  0.0 55.0 jit_solution(17784244515756155540)
XLA Ops:
  1.3 0.0 copy-start
  1.3 1.2 %copy-done = bf16[128,3584]{1,0:T(8,128)(2,1)S(1)} copy-done((bf16[128,3584]{1,0:T(8,128)(2,1)S(1)}, bf16[128,3584]{1,0:T(8,128)(2,1)}, u32[]{:S(2)}) %copy-start) | copy-done | bytes 917528
  2.5 0.0 copy-start.1
  2.5 0.9 %copy-done.1 = bf16[128,1024]{1,0:T(8,128)(2,1)S(1)} copy-done((bf16[128,1024]{1,0:T(8,128)(2,1)S(1)}, bf16[128,1024]{1,0:T(8,128)(2,1)}, u32[]{:S(2)}) %copy-start.1) | copy-done | bytes 262168
  3.4 0.0 copy-start.2
  3.4 0.7 %copy-done.2 = s32[128,1]{0,1:T(1,128)S(1)} copy-done((s32[128,1]{0,1:T(1,128)S(1)}, s32[128,1]{0,1:T(1,128)}, u32[]{:S(2)}) %copy-start.2) | copy-done | bytes 536
  4.1 0.0 copy-start.3
  4.1 0.7 %copy-done.3 = f32[128,1]{0,1:T(1,128)S(1)} copy-done((f32[128,1]{0,1:T(1,128)S(1)}, f32[128,1]{0,1:T(1,128)}, u32[]{:S(2)}) %copy-start.3) | copy-done | bytes 536
  4.7 48.1 %shard_map.85 = (bf16[128,1024]{1,0:T(8,128)(2,1)S(1)}, bf16[128,3584]{1,0:T(8,128)(2,1)S(1)}, f32[1,128]{1,0:T(1,128)S(1)}) custom-call(s32[1,128]{1,0:T(1,128)S(1)} %bitcast.3, f32[1,128]{1,0:T(1,128)S(1)} %bitcast.4, s32[1]{0:T(128)S(6)} %copy.12.counts_ref, bf16[128,3584]{1,0:T(8,128)(2,1)S(1)} %copy-done, bf16[1,3584,1024]{2,1,0:T(8,128)(2,1)} %weight_hbm.1, ...), custom_call_target="tpu_custom_call" | custom-call | tf_op jit(solution)/shard_map/pallas_call | solution.py:299
  52.8 0.7 %copy.13 = bf16[128,1024]{1,0:T(8,128)(2,1)} copy(bf16[128,1024]{1,0:T(8,128)(2,1)S(1)} %get-tuple-element.12) | data formatting | bytes 524288
  53.6 0.9 %copy.14 = bf16[128,3584]{1,0:T(8,128)(2,1)} copy(bf16[128,3584]{1,0:T(8,128)(2,1)S(1)} %get-tuple-element.13) | data formatting | bytes 1835008
  54.5 0.5 copy.15
Async XLA Ops:
  1.3 1.2 %copy-start = (bf16[128,3584]{1,0:T(8,128)(2,1)S(1)}, bf16[128,3584]{1,0:T(8,128)(2,1)}, u32[]{:S(2)}) copy-start(bf16[128,3584]{1,0:T(8,128)(2,1)} %tokens_hbm.1) | copy-start | bytes 2752516
  2.5 0.9 %copy-start.1 = (bf16[128,1024]{1,0:T(8,128)(2,1)S(1)}, bf16[128,1024]{1,0:T(8,128)(2,1)}, u32[]{:S(2)}) copy-start(bf16[128,1024]{1,0:T(8,128)(2,1)} %cotangent_hbm.1) | copy-start | bytes 786436
  3.4 0.7 %copy-start.2 = (s32[128,1]{0,1:T(1,128)S(1)}, s32[128,1]{0,1:T(1,128)}, u32[]{:S(2)}) copy-start(s32[128,1]{0,1:T(1,128)} %param.7) | copy-start | bytes 1540
  4.1 0.7 %copy-start.3 = (f32[128,1]{0,1:T(1,128)S(1)}, f32[128,1]{0,1:T(1,128)}, u32[]{:S(2)}) copy-start(f32[128,1]{0,1:T(1,128)} %param.8) | copy-start | bytes 1540

commit v2 on v1

--- a/solution.py
+++ b/solution.py
@@ -20,9 +20,9 @@
 
 
 def kernel(
-    n, groups, cap, routes_ref, gates_ref, counts_ref, tokens_hbm, weight_hbm, cotangent_hbm,
+    n, groups, cap, routes_hbm, gates_hbm, counts_ref, tokens_hbm, weight_hbm, cotangent_hbm,
     mixed_hbm, grad_hbm, gate_grad_ref,
-    tok, cot, w, place, unplace, tok_out, cot_out, tok_in, cot_in, delta,
+    routes_ref, gates_ref, tok, cot, w, place, unplace, tok_out, cot_out, tok_in, cot_in, delta,
     act_out, grad_out, act_home, grad_home, mixed_v, grad_v, cnt_mine, cnt_dp, cnt_sum, cnt_ex,
     load_sem, store_sem, send_sem, recv_sem, cnt_send, cnt_recv,
 ):
@@ -38,9 +38,12 @@
     load_tok = pltpu.make_async_copy(tokens_hbm, tok, load_sem.at[0])
     load_cot = pltpu.make_async_copy(cotangent_hbm, cot, load_sem.at[1])
     load_w = pltpu.make_async_copy(weight_hbm.at[0], w, load_sem.at[2])
+    load_routes = pltpu.make_async_copy(routes_hbm, routes_ref, load_sem.at[3])
+    load_gates = pltpu.make_async_copy(gates_hbm, gates_ref, load_sem.at[4])
+    load_routes.start()
+    load_gates.start()
     load_tok.start()
     load_cot.start()
-    load_w.start()
 
     barrier = pltpu.get_barrier_semaphore()
     for j in range(1, n):
@@ -52,6 +55,8 @@
             barrier, inc=1, device_id=(lax.rem(group + k, groups), me), device_id_type=MESH
         )
 
+    load_routes.wait()
+    load_gates.wait()
     route = routes_ref[...]
     high = -(-n // ROWS) * ROWS
     choose = lax.broadcasted_iota(jnp.int32, (high, rows), 0) == route
@@ -114,28 +119,34 @@
 
     out = []
 
-    load_tok.wait()
-    for part in range(pieces):
+    def send_far(part):
         gather(tok, tok_out, 2 * cap + part * step, step)
         if part == 0:
-            load_cot.wait()
             pl.semaphore_wait(barrier, n - 1 + groups - 1)
         for j in range(2, n):
             copy = remote(TOK, tok_out, tok_in, j, part, far_at(part, j), ROWS)
             copy.start()
             out.append(copy)
+        if part == 0:
+            load_cot.wait()
+            load_w.start()
         gather(cot, cot_out, 2 * cap + part * step, step)
         for j in range(2, n):
             copy = remote(COT, cot_out, cot_in, j, part, far_at(part, j), ROWS)
             copy.start()
             out.append(copy)
-        if part == 0:
-            gather(tok, tok_out, cap, cap)
-            near_tok = remote(TOK, tok_out, tok_in, 1, 0, cap, cap)
-            near_tok.start()
-            gather(cot, cot_out, cap, cap)
-            near_cot = remote(COT, cot_out, cot_in, 1, 0, cap, cap)
-            near_cot.start()
+
+    early = min(2, pieces)
+    load_tok.wait()
+    send_far(0)
+    gather(tok, tok_out, cap, cap)
+    near_tok = remote(TOK, tok_out, tok_in, 1, 0, cap, cap)
+    near_tok.start()
+    gather(cot, cot_out, cap, cap)
+    near_cot = remote(COT, cot_out, cot_in, 1, 0, cap, cap)
+    near_cot.start()
+    for part in range(1, early):
+        send_far(part)
 
     counts = []
     for k in range(1, groups):
@@ -199,6 +210,8 @@
     backward(0, 2 * cap, cap)
     near_grad = remote(GRAD, grad_out, grad_home, 1, 0, cap, cap)
     near_grad.start()
+    for part in range(early, pieces):
+        send_far(part)
 
     for copy in counts:
         copy.wait_recv()
@@ -303,9 +316,11 @@
                 jax.ShapeDtypeStruct((rows, depth), bf16),
                 jax.ShapeDtypeStruct((1, rows), jnp.float32),
             ),
-            in_specs=[vmem, vmem, pl.BlockSpec(memory_space=pltpu.SMEM), hbm, hbm, hbm],
+            in_specs=[hbm, hbm, pl.BlockSpec(memory_space=pltpu.SMEM), hbm, hbm, hbm],
             out_specs=(hbm, hbm, vmem),
             scratch_shapes=[
+                pltpu.VMEM((1, rows), jnp.int32),
+                pltpu.VMEM((1, rows), jnp.float32),
                 pltpu.VMEM((rows, depth), bf16),
                 pltpu.VMEM((rows, units), bf16),
                 pltpu.VMEM((depth, units), bf16),
@@ -326,7 +341,7 @@
                 pltpu.VMEM((groups - 1, 8, 128), jnp.float32),
                 pltpu.VMEM((8, 128), jnp.float32),
                 pltpu.VMEM((n - 1, 8, 128), jnp.float32),
-                pltpu.SemaphoreType.DMA((3,)),
+                pltpu.SemaphoreType.DMA((5,)),
                 pltpu.SemaphoreType.DMA((1 + depth // tile_of(depth, 512),)),
                 pltpu.SemaphoreType.DMA((4, n, pieces)),
                 pltpu.SemaphoreType.DMA((4, n, pieces)),
@@ -334,7 +349,7 @@
                 pltpu.SemaphoreType.DMA((groups - 1 + n - 1,)),
             ],
             compiler_params=pltpu.CompilerParams(
-                collective_id=0, has_side_effects=True, vmem_limit_bytes=48 * 1024 * 1024
+                collective_id=0, has_side_effects=True, vmem_limit_bytes=63 * 1024 * 1024
             ),
         )(routes.reshape(1, rows), gates.reshape(1, rows), counts, tokens, expert_weight, cotangent)
         return (mixed, token_grad, gate_grad.reshape(rows, 1))

time: 55.2 us -> 54.7 us (level)
  local copies, waits for them, and re-layouts: 5.57 us -> 4.96 us
    unnamed x11 -> x3, local copies, waits for them, and re-layouts: 5.57 us -> 4.96 us
where the time goes in v2:
time: 54.7 us; the launch traced here: 54.4 us
  Pallas kernels  48.2 us (88%)
  local copies, waits for them, and re-layouts  4.96 us (9%)
  between operations  1.29 us (2%)
    pallas_call x1, Pallas kernels, shards(): pl.pallas_call(functools.partial(kernel, n, groups, cap), out_shape=(jax....  48.2 us
    unnamed x3, local copies, waits for them, and re-layouts  4.96 us

profile of v2, /device:TPU:1, one launch (start us, length us, event | category | flops | bytes accessed | tf_op | source)
XLA Modules:
  0.0 54.4 jit_solution(16283065765218383704)
XLA Ops:
  1.3 48.2 %shard_map.85 = (bf16[128,1024]{1,0:T(8,128)(2,1)}, bf16[128,3584]{1,0:T(8,128)(2,1)}, f32[1,128]{1,0:T(1,128)}) custom-call(s32[1,128]{1,0:T(1,128)} %bitcast.3, f32[1,128]{1,0:T(1,128)} %bitcast.4, s32[1]{0:T(128)S(6)} %copy.12.counts_ref, bf16[128,3584]{1,0:T(8,128)(2,1)} %tokens_hbm.1, bf16[1,3584,1024]{2,1,0:T(8,128)(2,1)} %weight_hbm.1, ...), custom_call_target="tpu_custom_call" | custom-call | tf_op jit(solution)/shard_map/pallas_call | solution.py:312
  49.5 1.7 %copy.13 = bf16[128,1024]{1,0:T(8,128)(2,1)} copy(bf16[128,1024]{1,0:T(8,128)(2,1)} %get-tuple-element.12) | data formatting | bytes 524288
  51.2 2.2 %copy.14 = bf16[128,3584]{1,0:T(8,128)(2,1)} copy(bf16[128,3584]{1,0:T(8,128)(2,1)} %get-tuple-element.13) | data formatting | bytes 1835008
  53.3 1.1 %copy.15 = f32[128,1]{0,1:T(1,128)} copy(f32[128,1]{0,1:T(1,128)} %bitcast.5) | data formatting | bytes 1024

commit v3 on v2

--- a/solution.py
+++ b/solution.py
@@ -21,10 +21,10 @@
 
 def kernel(
     n, groups, cap, routes_hbm, gates_hbm, counts_ref, tokens_hbm, weight_hbm, cotangent_hbm,
-    mixed_hbm, grad_hbm, gate_grad_ref,
-    routes_ref, gates_ref, tok, cot, w, place, unplace, tok_out, cot_out, tok_in, cot_in, delta,
-    act_out, grad_out, act_home, grad_home, mixed_v, grad_v, cnt_mine, cnt_dp, cnt_sum, cnt_ex,
-    load_sem, store_sem, send_sem, recv_sem, cnt_send, cnt_recv,
+    act_home, grad_home, unplace, columns_ref,
+    routes_ref, gates_ref, tok, cot, w, place, tok_out, cot_out, tok_in, cot_in, delta,
+    act_out, grad_out, cnt_mine, cnt_dp, cnt_sum, cnt_ex,
+    load_sem, send_sem, recv_sem, cnt_send, cnt_recv,
 ):
     rows, depth = tok.shape
     units = cot.shape[1]
@@ -164,7 +164,7 @@
     gather(tok, tok_in, 0, cap)
     gather(cot, cot_in, 0, cap)
 
-    def forward(at, size, kept):
+    def forward(at, size):
         width = tile_of(units, 256)
 
         def body(i, carry):
@@ -174,9 +174,7 @@
             )
             sig = jax.nn.sigmoid(pre)
             act = (pre * sig).astype(jnp.bfloat16)
-            if kept:
-                act_home[at : at + kept, cut] = act[:kept]
-            act_out[at + kept : at + size, cut] = act[kept:]
+            act_out[at : at + size, cut] = act
             slope = sig * (1.0 + pre * (1.0 - sig))
             delta[0:size, cut] = (
                 cot_in[at : at + size, cut].astype(jnp.float32) * slope
@@ -185,7 +183,7 @@
 
         lax.fori_loop(0, units // width, body, 0)
 
-    def backward(at, size, kept):
+    def backward(at, size):
         width = tile_of(depth, 512)
 
         def body(i, carry):
@@ -194,9 +192,7 @@
                 delta[0:size, :], w[cut, :], (((1,), (1,)), ((), ())),
                 preferred_element_type=jnp.float32,
             ).astype(jnp.bfloat16)
-            if kept:
-                grad_home[at : at + kept, cut] = grad[:kept]
-            grad_out[at + kept : at + size, cut] = grad[kept:]
+            grad_out[at : at + size, cut] = grad
             return carry
 
         lax.fori_loop(0, depth // width, body, 0)
@@ -204,12 +200,20 @@
     load_w.wait()
     near_tok.wait_recv()
     near_cot.wait_recv()
-    forward(0, 2 * cap, cap)
+    forward(0, 2 * cap)
     near_act = remote(ACT, act_out, act_home, 1, 0, cap, cap)
     near_act.start()
-    backward(0, 2 * cap, cap)
+    own_act = pltpu.make_async_copy(
+        act_out.at[pl.ds(0, cap)], act_home.at[pl.ds(0, cap)], load_sem.at[0]
+    )
+    own_act.start()
+    backward(0, 2 * cap)
     near_grad = remote(GRAD, grad_out, grad_home, 1, 0, cap, cap)
     near_grad.start()
+    own_grad = pltpu.make_async_copy(
+        grad_out.at[pl.ds(0, cap)], grad_home.at[pl.ds(0, cap)], load_sem.at[1]
+    )
+    own_grad.start()
     for part in range(early, pieces):
         send_far(part)
 
@@ -240,11 +244,11 @@
                     remote(TOK, tok_out, tok_in, j, part, far_at(part, j), ROWS).wait_recv()
                 else:
                     remote(COT, cot_out, cot_in, j, part, far_at(part, j), ROWS).wait_recv()
-        forward(at, step, 0)
+        forward(at, step)
         for j in range(2, n):
             copy = remote(ACT, act_out, act_home, j, part, far_at(part, j), ROWS)
             copy.start()
-        backward(at, step, 0)
+        backward(at, step)
         for j in range(2, n):
             copy = remote(GRAD, grad_out, grad_home, j, part, far_at(part, j), ROWS)
             copy.start()
@@ -264,22 +268,29 @@
     position = lax.broadcasted_iota(jnp.int32, (rows, 1), 0)
     factor = jnp.where(position < count, 1.0, 0.0) * scale
 
+    lane = lax.broadcasted_iota(jnp.int32, (rows, 128), 1)
+    columns_ref[...] = jnp.where(
+        lane == 0, gate, jnp.where(lane == 1, gate * factor, factor)
+    )
+
+    own_act.wait()
+    own_grad.wait()
     near_act.wait()
+    near_grad.wait()
     for part in range(pieces):
         for j in range(2, n):
             remote(ACT, act_out, act_home, j, part, far_at(part, j), ROWS).wait()
-    act = jnp.dot(unplace[...], act_home[...], preferred_element_type=jnp.float32)
-    mixed_v[...] = (gate * act).astype(jnp.bfloat16)
-    store_mixed = pltpu.make_async_copy(mixed_v, mixed_hbm, store_sem.at[0])
-    store_mixed.start()
-    dots = jnp.sum(act * cot[...].astype(jnp.float32), axis=1, keepdims=True) * factor
-    gate_grad_ref[...] = jnp.transpose(jnp.broadcast_to(dots, (rows, 128)))[0:1, :]
-
-    near_grad.wait()
-    for part in range(pieces):
-        for j in range(2, n):
             remote(GRAD, grad_out, grad_home, j, part, far_at(part, j), ROWS).wait()
-    both = gate * factor
+
+
+def finish(
+    act_home, grad_home, unplace, columns, cotangent_hbm,
+    mixed_hbm, grad_hbm, gate_grad_ref, cot, mixed_v, grad_v, load_sem, store_sem,
+):
+    rows, depth = grad_v.shape
+    load_cot = pltpu.make_async_copy(cotangent_hbm, cot, load_sem.at[0])
+    load_cot.start()
+    both = columns[:, 1:2]
     width = tile_of(depth, 512)
     stores = []
     for i in range(depth // width):
@@ -290,9 +301,20 @@
         store = pltpu.make_async_copy(grad_v.at[:, cut], grad_hbm.at[:, cut], store_sem.at[1 + i])
         store.start()
         stores.append(store)
+    act = jnp.dot(unplace[...], act_home[...], preferred_element_type=jnp.float32)
+    mixed_v[...] = (columns[:, 0:1] * act).astype(jnp.bfloat16)
+    store_mixed = pltpu.make_async_copy(mixed_v, mixed_hbm, store_sem.at[0])
+    store_mixed.start()
+    load_cot.wait()
+    dots = jnp.sum(act * cot[...].astype(jnp.float32), axis=1, keepdims=True) * columns[:, 2:3]
+    gate_grad_ref[...] = jnp.transpose(jnp.broadcast_to(dots, (rows, 128)))[0:1, :]
     store_mixed.wait()
     for store in stores:
         store.wait()
+
+
+def pinned(array):
+    return pltpu.with_memory_space_constraint(array, pltpu.HBM)
 
 
 def solution(mesh):
@@ -307,17 +329,20 @@
         pieces = cap // ROWS
         small = max(2 * cap, (n - 2) * ROWS)
         bf16 = jnp.bfloat16
-        hbm = pl.BlockSpec(memory_space=pl.ANY)
+        hbm = pl.BlockSpec(memory_space=pltpu.HBM)
+        held = pinned(cotangent)
+        free = pl.BlockSpec(memory_space=pl.ANY)
         vmem = pl.BlockSpec(memory_space=pltpu.VMEM)
-        mixed, token_grad, gate_grad = pl.pallas_call(
+        act_home, grad_home, unplace, columns = pl.pallas_call(
             functools.partial(kernel, n, groups, cap),
             out_shape=(
-                jax.ShapeDtypeStruct((rows, units), bf16),
-                jax.ShapeDtypeStruct((rows, depth), bf16),
-                jax.ShapeDtypeStruct((1, rows), jnp.float32),
+                jax.ShapeDtypeStruct((slots, units), bf16),
+                jax.ShapeDtypeStruct((slots, depth), bf16),
+                jax.ShapeDtypeStruct((rows, slots), bf16),
+                jax.ShapeDtypeStruct((rows, 128), jnp.float32),
             ),
             in_specs=[hbm, hbm, pl.BlockSpec(memory_space=pltpu.SMEM), hbm, hbm, hbm],
-            out_specs=(hbm, hbm, vmem),
+            out_specs=(free, free, vmem, vmem),
             scratch_shapes=[
                 pltpu.VMEM((1, rows), jnp.int32),
                 pltpu.VMEM((1, rows), jnp.float32),
@@ -325,7 +350,6 @@
                 pltpu.VMEM((rows, units), bf16),
                 pltpu.VMEM((depth, units), bf16),
                 pltpu.VMEM((slots, rows), bf16),
-                pltpu.VMEM((rows, slots), bf16),
                 pltpu.VMEM((slots, depth), bf16),
                 pltpu.VMEM((slots, units), bf16),
                 pltpu.VMEM((slots, depth), bf16),
@@ -333,25 +357,45 @@
                 pltpu.VMEM((small, units), bf16),
                 pltpu.VMEM((slots, units), bf16),
                 pltpu.VMEM((slots, depth), bf16),
-                pltpu.VMEM((slots, units), bf16),
-                pltpu.VMEM((slots, depth), bf16),
-                pltpu.VMEM((rows, units), bf16),
-                pltpu.VMEM((rows, depth), bf16),
                 pltpu.VMEM((8, 128), jnp.float32),
                 pltpu.VMEM((groups - 1, 8, 128), jnp.float32),
                 pltpu.VMEM((8, 128), jnp.float32),
                 pltpu.VMEM((n - 1, 8, 128), jnp.float32),
                 pltpu.SemaphoreType.DMA((5,)),
-                pltpu.SemaphoreType.DMA((1 + depth // tile_of(depth, 512),)),
                 pltpu.SemaphoreType.DMA((4, n, pieces)),
                 pltpu.SemaphoreType.DMA((4, n, pieces)),
                 pltpu.SemaphoreType.DMA((groups - 1 + n - 1,)),
                 pltpu.SemaphoreType.DMA((groups - 1 + n - 1,)),
             ],
             compiler_params=pltpu.CompilerParams(
-                collective_id=0, has_side_effects=True, vmem_limit_bytes=63 * 1024 * 1024
+                collective_id=0, has_side_effects=True, vmem_limit_bytes=40 * 1024 * 1024
             ),
-        )(routes.reshape(1, rows), gates.reshape(1, rows), counts, tokens, expert_weight, cotangent)
+        )(
+            pinned(routes.reshape(1, rows)),
+            pinned(gates.reshape(1, rows)),
+            counts,
+            pinned(tokens),
+            pinned(expert_weight),
+            held,
+        )
+        mixed, token_grad, gate_grad = pl.pallas_call(
+            finish,
+            out_shape=(
+                jax.ShapeDtypeStruct((rows, units), bf16),
+                jax.ShapeDtypeStruct((rows, depth), bf16),
+                jax.ShapeDtypeStruct((1, rows), jnp.float32),
+            ),
+            in_specs=[vmem, vmem, vmem, vmem, hbm],
+            out_specs=(hbm, hbm, vmem),
+            scratch_shapes=[
+                pltpu.VMEM((rows, units), bf16),
+                pltpu.VMEM((rows, units), bf16),
+                pltpu.VMEM((rows, depth), bf16),
+                pltpu.SemaphoreType.DMA((1,)),
+                pltpu.SemaphoreType.DMA((1 + depth // tile_of(depth, 512),)),
+            ],
+            compiler_params=pltpu.CompilerParams(vmem_limit_bytes=24 * 1024 * 1024),
+        )(act_home, grad_home, unplace, columns, held)
         return (mixed, token_grad, gate_grad.reshape(rows, 1))
 
     spread = P(("dp", "expert"), None)

time: 54.7 us -> 50 us (0.914)
  local copies, waits for them, and re-layouts: 4.96 us -> 0 us
    unnamed x3 -> x0, local copies, waits for them, and re-layouts: 4.96 us -> none
    pallas_call x0 -> x1, Pallas kernels: none -> 2.05 us  [shards(): pl.pallas_call(finish, out_shape=(jax.ShapeDtypeStruct((rows, units), bf1...]
    pallas_call x1, Pallas kernels: 48.2 us -> 46.5 us  [shards(): pl.pallas_call(functools.partial(kernel, n, groups, cap), out_shape=(jax....]
where the time goes in v3:
time: 50 us; the launch traced here: 49.8 us
  Pallas kernels  48.5 us (97%)
  between operations  1.29 us (3%)
    pallas_call x1, Pallas kernels, shards(): pl.pallas_call(functools.partial(kernel, n, groups, cap), out_shape=(jax....  46.5 us
    pallas_call x1, Pallas kernels, shards(): pl.pallas_call(finish, out_shape=(jax.ShapeDtypeStruct((rows, units), bf1...  2.05 us

profile of v3, /device:TPU:1, one launch (start us, length us, event | category | flops | bytes accessed | tf_op | source)
XLA Modules:
  0.0 49.8 jit_solution(12576334838928126113)
XLA Ops:
  1.3 46.5 %shard_map.85 = (bf16[192,1024]{1,0:T(8,128)(2,1)S(1)}, bf16[192,3584]{1,0:T(8,128)(2,1)S(1)}, bf16[128,192]{1,0:T(8,128)(2,1)S(1)}, f32[128,128]{1,0:T(8,128)S(1)}) custom-call(s32[1,128]{1,0:T(1,128)} %bitcast.3, f32[1,128]{1,0:T(1,128)} %bitcast.4, s32[1]{0:T(128)S(6)} %copy.9.counts_ref, bf16[128,3584]{1,0:T(8,128)(2,1)} %tokens_hbm.1, ...), custom_call_target="tpu_custom_call" | custom-call | tf_op jit(solution)/shard_map/pallas_call | solution.py:336
  47.8 2.0 %shard_map.86 = (bf16[128,1024]{1,0:T(8,128)(2,1)}, bf16[128,3584]{1,0:T(8,128)(2,1)}, f32[1,128]{1,0:T(1,128)}) custom-call(bf16[192,1024]{1,0:T(8,128)(2,1)S(1)} %get-tuple-element.10.act_home, bf16[192,3584]{1,0:T(8,128)(2,1)S(1)} %get-tuple-element.11.grad_home, bf16[128,192]{1,0:T(8,128)(2,1)S(1)} %get-tuple-element.12.unplace, ...), custom_call_target="tpu_custom_call" | custom-call | tf_op jit(solution)/shard_map/pallas_call | solution.py:381

commit v4 on v3

--- a/solution.py
+++ b/solution.py
@@ -21,9 +21,9 @@
 
 def kernel(
     n, groups, cap, routes_hbm, gates_hbm, counts_ref, tokens_hbm, weight_hbm, cotangent_hbm,
-    act_home, grad_home, unplace, columns_ref,
+    mixed_ref, gate_grad_ref, grad_home, unplace, columns_ref,
     routes_ref, gates_ref, tok, cot, w, place, tok_out, cot_out, tok_in, cot_in, delta,
-    act_out, grad_out, cnt_mine, cnt_dp, cnt_sum, cnt_ex,
+    act_out, act_home, grad_out, cnt_mine, cnt_dp, cnt_sum, cnt_ex,
     load_sem, send_sem, recv_sem, cnt_send, cnt_recv,
 ):
     rows, depth = tok.shape
@@ -35,6 +35,16 @@
     me = lax.axis_index("expert")
     group = lax.axis_index("dp")
 
+    barrier = pltpu.get_barrier_semaphore()
+    for j in range(1, n):
+        pl.semaphore_signal(
+            barrier, inc=1, device_id=(group, lax.bitwise_xor(me, j)), device_id_type=MESH
+        )
+    for k in range(1, groups):
+        pl.semaphore_signal(
+            barrier, inc=1, device_id=(lax.rem(group + k, groups), me), device_id_type=MESH
+        )
+
     load_tok = pltpu.make_async_copy(tokens_hbm, tok, load_sem.at[0])
     load_cot = pltpu.make_async_copy(cotangent_hbm, cot, load_sem.at[1])
     load_w = pltpu.make_async_copy(weight_hbm.at[0], w, load_sem.at[2])
@@ -44,16 +54,6 @@
     load_gates.start()
     load_tok.start()
     load_cot.start()
-
-    barrier = pltpu.get_barrier_semaphore()
-    for j in range(1, n):
-        pl.semaphore_signal(
-            barrier, inc=1, device_id=(group, lax.bitwise_xor(me, j)), device_id_type=MESH
-        )
-    for k in range(1, groups):
-        pl.semaphore_signal(
-            barrier, inc=1, device_id=(lax.rem(group + k, groups), me), device_id_type=MESH
-        )
 
     load_routes.wait()
     load_gates.wait()
@@ -270,27 +270,34 @@
 
     lane = lax.broadcasted_iota(jnp.int32, (rows, 128), 1)
     columns_ref[...] = jnp.where(
-        lane == 0, gate, jnp.where(lane == 1, gate * factor, factor)
+        lane == 0, gate * factor, 0.0
     )
 
     own_act.wait()
+    near_act.wait()
+    for part in range(pieces):
+        for j in range(2, n):
+            remote(ACT, act_out, act_home, j, part, far_at(part, j), ROWS).wait()
+    act = jnp.dot(unplace[...], act_home[...], preferred_element_type=jnp.float32)
+    mixed_ref[...] = (gate * act).astype(jnp.bfloat16)
+    dots = jnp.sum(act * cot[...].astype(jnp.float32), axis=1, keepdims=True) * factor
+    gate_grad_ref[...] = jnp.transpose(jnp.broadcast_to(dots, (rows, 128)))[0:1, :]
+
     own_grad.wait()
-    near_act.wait()
     near_grad.wait()
     for part in range(pieces):
         for j in range(2, n):
-            remote(ACT, act_out, act_home, j, part, far_at(part, j), ROWS).wait()
             remote(GRAD, grad_out, grad_home, j, part, far_at(part, j), ROWS).wait()
 
 
 def finish(
-    act_home, grad_home, unplace, columns, cotangent_hbm,
-    mixed_hbm, grad_hbm, gate_grad_ref, cot, mixed_v, grad_v, load_sem, store_sem,
+    mixed, gate_grad, grad_home, unplace, columns,
+    mixed_hbm, grad_hbm, gate_grad_ref, grad_v, store_sem,
 ):
-    rows, depth = grad_v.shape
-    load_cot = pltpu.make_async_copy(cotangent_hbm, cot, load_sem.at[0])
-    load_cot.start()
-    both = columns[:, 1:2]
+    depth = grad_v.shape[1]
+    store_mixed = pltpu.make_async_copy(mixed, mixed_hbm, store_sem.at[0])
+    store_mixed.start()
+    both = columns[:, 0:1]
     width = tile_of(depth, 512)
     stores = []
     for i in range(depth // width):
@@ -301,13 +308,7 @@
         store = pltpu.make_async_copy(grad_v.at[:, cut], grad_hbm.at[:, cut], store_sem.at[1 + i])
         store.start()
         stores.append(store)
-    act = jnp.dot(unplace[...], act_home[...], preferred_element_type=jnp.float32)
-    mixed_v[...] = (columns[:, 0:1] * act).astype(jnp.bfloat16)
-    store_mixed = pltpu.make_async_copy(mixed_v, mixed_hbm, store_sem.at[0])
-    store_mixed.start()
-    load_cot.wait()
-    dots = jnp.sum(act * cot[...].astype(jnp.float32), axis=1, keepdims=True) * columns[:, 2:3]
-    gate_grad_ref[...] = jnp.transpose(jnp.broadcast_to(dots, (rows, 128)))[0:1, :]
+    gate_grad_ref[...] = gate_grad[...]
     store_mixed.wait()
     for store in stores:
         store.wait()
@@ -330,19 +331,19 @@
         small = max(2 * cap, (n - 2) * ROWS)
         bf16 = jnp.bfloat16
         hbm = pl.BlockSpec(memory_space=pltpu.HBM)
-        held = pinned(cotangent)
         free = pl.BlockSpec(memory_space=pl.ANY)
         vmem = pl.BlockSpec(memory_space=pltpu.VMEM)
-        act_home, grad_home, unplace, columns = pl.pallas_call(
+        mixed, gate_grad, grad_home, unplace, columns = pl.pallas_call(
             functools.partial(kernel, n, groups, cap),
             out_shape=(
-                jax.ShapeDtypeStruct((slots, units), bf16),
+                jax.ShapeDtypeStruct((rows, units), bf16),
+                jax.ShapeDtypeStruct((1, rows), jnp.float32),
                 jax.ShapeDtypeStruct((slots, depth), bf16),
                 jax.ShapeDtypeStruct((rows, slots), bf16),
                 jax.ShapeDtypeStruct((rows, 128), jnp.float32),
             ),
             in_specs=[hbm, hbm, pl.BlockSpec(memory_space=pltpu.SMEM), hbm, hbm, hbm],
-            out_specs=(free, free, vmem, vmem),
+            out_specs=(vmem, vmem, free, vmem, vmem),
             scratch_shapes=[
                 pltpu.VMEM((1, rows), jnp.int32),
                 pltpu.VMEM((1, rows), jnp.float32),
@@ -355,6 +356,7 @@
                 pltpu.VMEM((slots, depth), bf16),
                 pltpu.VMEM((slots, units), bf16),
                 pltpu.VMEM((small, units), bf16),
+                pltpu.VMEM((slots, units), bf16),
                 pltpu.VMEM((slots, units), bf16),
                 pltpu.VMEM((slots, depth), bf16),
                 pltpu.VMEM((8, 128), jnp.float32),
@@ -376,7 +378,7 @@
             counts,
             pinned(tokens),
             pinned(expert_weight),
-            held,
+            pinned(cotangent),
         )
         mixed, token_grad, gate_grad = pl.pallas_call(
             finish,
@@ -385,17 +387,14 @@
                 jax.ShapeDtypeStruct((rows, depth), bf16),
                 jax.ShapeDtypeStruct((1, rows), jnp.float32),
             ),
-            in_specs=[vmem, vmem, vmem, vmem, hbm],
+            in_specs=[vmem, vmem, vmem, vmem, vmem],
             out_specs=(hbm, hbm, vmem),
             scratch_shapes=[
-                pltpu.VMEM((rows, units), bf16),
-                pltpu.VMEM((rows, units), bf16),
                 pltpu.VMEM((rows, depth), bf16),
-                pltpu.SemaphoreType.DMA((1,)),
                 pltpu.SemaphoreType.DMA((1 + depth // tile_of(depth, 512),)),
             ],
             compiler_params=pltpu.CompilerParams(vmem_limit_bytes=24 * 1024 * 1024),
-        )(act_home, grad_home, unplace, columns, held)
+        )(mixed, gate_grad, grad_home, unplace, columns)
         return (mixed, token_grad, gate_grad.reshape(rows, 1))
 
     spread = P(("dp", "expert"), None)

time: 50 us -> 49.6 us (level)
  no operation moved by 1% of the time
where the time goes in v4:
time: 49.6 us; the launch traced here: 49.5 us
  Pallas kernels  48.2 us (97%)
  between operations  1.29 us (3%)
    pallas_call x1, Pallas kernels, shards(): pl.pallas_call(functools.partial(kernel, n, groups, cap), out_shape=(jax....  46.5 us
    pallas_call x1, Pallas kernels, shards(): pl.pallas_call(finish, out_shape=(jax.ShapeDtypeStruct((rows, units), bf1...  1.71 us

profile of v4, /device:TPU:1, one launch (start us, length us, event | category | flops | bytes accessed | tf_op | source)
XLA Modules:
  0.0 49.5 jit_solution(2001130697516004864)
XLA Ops:
  1.3 46.5 %shard_map.85 = (bf16[128,1024]{1,0:T(8,128)(2,1)S(1)}, f32[1,128]{1,0:T(1,128)S(1)}, bf16[192,3584]{1,0:T(8,128)(2,1)S(1)}, bf16[128,192]{1,0:T(8,128)(2,1)S(1)}, f32[128,128]{1,0:T(8,128)S(1)}) custom-call(s32[1,128]{1,0:T(1,128)} %bitcast.3, f32[1,128]{1,0:T(1,128)} %bitcast.4, s32[1]{0:T(128)S(6)} %copy.9.counts_ref, bf16[128,3584]{1,0:T(8,128)(2,1)} %tokens_hbm.1, ...), custom_call_target="tpu_custom_call" | custom-call | tf_op jit(solution)/shard_map/pallas_call | solution.py:336
  47.8 1.7 %shard_map.86 = (bf16[128,1024]{1,0:T(8,128)(2,1)}, bf16[128,3584]{1,0:T(8,128)(2,1)}, f32[1,128]{1,0:T(1,128)}) custom-call(bf16[128,1024]{1,0:T(8,128)(2,1)S(1)} %get-tuple-element.11.mixed, f32[1,128]{1,0:T(1,128)S(1)} %get-tuple-element.12.gate_grad, bf16[192,3584]{1,0:T(8,128)(2,1)S(1)} %get-tuple-element.13.grad_home, ...), custom_call_target="tpu_custom_call" | custom-call | tf_op jit(solution)/shard_map/pallas_call | solution.py:383

commit v5 on v4

--- a/solution.py
+++ b/solution.py
@@ -136,7 +136,7 @@
             copy.start()
             out.append(copy)
 
-    early = min(2, pieces)
+    early = pieces
     load_tok.wait()
     send_far(0)
     gather(tok, tok_out, cap, cap)

time: 49.6 us -> 49.6 us (level)
  no operation moved by 1% of the time
where the time goes in v5:
time: 49.6 us; the launch traced here: 49.5 us
  Pallas kernels  48.2 us (97%)
  between operations  1.29 us (3%)
    pallas_call x1, Pallas kernels, shards(): pl.pallas_call(functools.partial(kernel, n, groups, cap), out_shape=(jax....  46.5 us
    pallas_call x1, Pallas kernels, shards(): pl.pallas_call(finish, out_shape=(jax.ShapeDtypeStruct((rows, units), bf1...  1.71 us

profile of v5, /device:TPU:1, one launch (start us, length us, event | category | flops | bytes accessed | tf_op | source)
XLA Modules:
  0.0 49.5 jit_solution(14032663024123611358)
XLA Ops:
  1.3 46.5 %shard_map.85 = (bf16[128,1024]{1,0:T(8,128)(2,1)S(1)}, f32[1,128]{1,0:T(1,128)S(1)}, bf16[192,3584]{1,0:T(8,128)(2,1)S(1)}, bf16[128,192]{1,0:T(8,128)(2,1)S(1)}, f32[128,128]{1,0:T(8,128)S(1)}) custom-call(s32[1,128]{1,0:T(1,128)} %bitcast.3, f32[1,128]{1,0:T(1,128)} %bitcast.4, s32[1]{0:T(128)S(6)} %copy.9.counts_ref, bf16[128,3584]{1,0:T(8,128)(2,1)} %tokens_hbm.1, ...), custom_call_target="tpu_custom_call" | custom-call | tf_op jit(solution)/shard_map/pallas_call | solution.py:336
  47.8 1.7 %shard_map.86 = (bf16[128,1024]{1,0:T(8,128)(2,1)}, bf16[128,3584]{1,0:T(8,128)(2,1)}, f32[1,128]{1,0:T(1,128)}) custom-call(bf16[128,1024]{1,0:T(8,128)(2,1)S(1)} %get-tuple-element.11.mixed, f32[1,128]{1,0:T(1,128)S(1)} %get-tuple-element.12.gate_grad, bf16[192,3584]{1,0:T(8,128)(2,1)S(1)} %get-tuple-element.13.grad_home, ...), custom_call_target="tpu_custom_call" | custom-call | tf_op jit(solution)/shard_map/pallas_call | solution.py:383
